TPU v7x, 32 devices: a whole 2x2x4 slice. The times are simulated.
32 devices in a mesh: rep: 2 (over x), lat: 16 (over z, y, core).
Axes of the slice: x: 2, y: 2, z: 4, core: 2. Of those that a mesh axis runs over, the one named last changes fastest.
Arguments:
- residuals: bfloat16 [512, 2, 3584], P(('rep', 'lat')), parts along dimension 0, may hold values from -6 to 6
- enc_weight: bfloat16 [2, 3584, 16384], P(None, None, 'lat'), may hold values from -0.09375 to 0.09375
- enc_bias: float32 [2, 16384], P(None, 'lat'), may hold values from -1 to 0.5
- dec_weight: bfloat16 [3, 16384, 3584], P(None, 'lat'), may hold values from -0.125 to 0.125
- dec_bias: float32 [2, 3584], replicated, may hold values from -3 to 3
- active_blocks: int32 [4, 4, 32], P('rep'), parts along dimension 0, may hold values from 0 to 127, as said below
- active_counts: int32 [4, 4], P('rep'), parts along dimension 0, may hold values from 1 to 32, as said below
Outputs:
- recon: bfloat16 [512, 2, 3584], P(('rep', 'lat')), parts along dimension 0
There are 2 independent parts, one for each index of `rep`. A program takes and returns all parts, laid end to end along the dimension named above; an argument that names none is the same for every part. Nothing has to cross between parts.
Inputs may be any that keep to these rules, and one draw needn't show every extreme that they name: `active_blocks`: the first active_counts entries of each layer's tile list are distinct latent blocks; later entries are to be ignored. `active_counts`: some layer's tile uses all 32 entries.
All inputs are finite; a program needn't handle non-finite values.
Results may differ from a plain program's by a relative error of at most 0.0046.
Values may be sent and summed in bfloat16 or wider, within the bound.
A program may use at most 128 MiB of HBM per device.

v0:
```python
import jax
import jax.numpy as jnp
from jax import lax
from jax.sharding import PartitionSpec as P

BLOCK = 128
LAYERS = 2
TILE = 64


def pair_index(source, target):
    return source * LAYERS - source * (source - 1) // 2 + target - source


def block_table(active_blocks, active_counts, blocks_here):
    holder = lax.axis_index("lat")
    block_ids = holder * blocks_here + jnp.arange(blocks_here, dtype=jnp.int32)
    in_list = (
        jnp.arange(active_blocks.shape[2], dtype=jnp.int32)[None, None, :]
        < active_counts[:, :, None]
    )
    matched = (active_blocks[..., None] == block_ids) & in_list[..., None]
    return jnp.any(matched, axis=2).astype(jnp.float32)


def encode(fragment, enc_weight, enc_bias, table):
    row_count = fragment.shape[0]
    lat_here = enc_weight.shape[2]
    blocks_here = lat_here // BLOCK
    preact = jnp.einsum("rld,ldk->rlk", fragment, enc_weight, preferred_element_type=jnp.float32)
    preact = preact + enc_bias[None, :, :]
    tile_of = jnp.arange(row_count, dtype=jnp.int32) // TILE
    one_hot = (tile_of[:, None] == jnp.arange(table.shape[1], dtype=jnp.int32)[None, :]).astype(
        jnp.float32
    )
    keep_rows = jnp.einsum("rt,ltj->rlj", one_hot, table)
    activation = (
        jax.nn.relu(preact).reshape(row_count, LAYERS, blocks_here, BLOCK) * keep_rows[..., None]
    )
    return activation.reshape(row_count, LAYERS, lat_here).astype(jnp.bfloat16)


def layer_term(latent_codes, dec_weight, target, amount):
    summed = jnp.zeros((amount, dec_weight.shape[2]), jnp.float32)
    for source in range(target + 1):
        summed = summed + jnp.dot(
            latent_codes[:, source, :],
            dec_weight[pair_index(source, target)],
            preferred_element_type=jnp.float32,
        )
    return summed


def body(residuals, enc_weight, enc_bias, dec_weight, dec_bias, active_blocks, active_counts):
    blocks_here = enc_weight.shape[2] // BLOCK
    table = block_table(active_blocks, active_counts, blocks_here)
    latent_codes = encode(
        lax.all_gather(residuals, "lat", axis=0, tiled=True), enc_weight, enc_bias, table
    )
    own_rows = latent_codes.shape[0] // lax.axis_size("lat")
    layers_out = []
    for target in range(LAYERS):
        layers_out.append(
            lax.psum_scatter(
                layer_term(latent_codes, dec_weight, target, own_rows * lax.axis_size("lat")),
                "lat",
                scatter_dimension=0,
                tiled=True,
            )
        )
    summed = jnp.stack(layers_out, axis=1)
    return (summed + dec_bias[None, :, :]).astype(jnp.bfloat16)


def solution(mesh):
    return jax.shard_map(
        body,
        mesh=mesh,
        in_specs=(
            P(("rep", "lat"), None, None),
            P(None, None, "lat"),
            P(None, "lat"),
            P(None, "lat", None),
            P(),
            P("rep", None, None),
            P("rep", None),
        ),
        out_specs=P(("rep", "lat"), None, None),
        check_vma=False,
    )
```

profile of v0, /device:TPU:0, one launch (start us, length us, event | category | flops | bytes accessed | tf_op | source)
XLA Modules:
  0.0 230.6 jit_solution(2741598272282128181)
XLA Ops:
  6.5 0.0 all-gather.2.cloned.1.call-start
  6.5 1.6 copy.11
  8.2 0.0 all-gather.2.cloned.1.call-update
  8.2 0.0 reduce-scatter.5.cloned.1.call-start
  8.3 0.8 iota_compare_fusion
  9.0 1.0 and_reduce_fusion
  10.0 0.2 fusion.15
  10.2 49.7 %all-gather.2.cloned.1.call-done = bf16[256,2,3584]{2,0,1:T(8,128)(2,1)} async-done(((bf16[16,2,3584]{2,0,1:T(8,128)(2,1)}), bf16[256,2,3584]{2,0,1:T(8,128)(2,1)}) %all-gather.2.cloned.1.call-update) | async-done | bytes 3670032 | tf_op jit(solution)/shard_map/all_gather | solution.py:58
  59.9 10.2 %fusion.12 = bf16[256,2,1024]{0,2,1:T(8,128)(2,1)S(1)} fusion(bf16[2,3584,1024]{2,1,0:T(8,128)(2,1)} %param.8, bf16[256,2,3584]{2,0,1:T(8,128)(2,1)} %all-gather.2.cloned.1.call-done, f32[256,2,8]{0,2,1:T(8,128)S(1)} %fusion.15, f32[2,1024]{1,0:T(2,128)} %param.9), kind=kOutput, calls=%fused_computation.11 | convolution fusion | flops 3760193536 | bytes 19423232 | tf_op jit(solution)/shard_map/rld,ldk->rlk/dot_general | solution.py:30
  70.2 5.2 %fusion = f32[256,3584]{1,0:T(8,128)S(1)} fusion(bf16[3,1024,3584]{2,1,0:T(8,128)(2,1)} %param.10, bf16[256,2,1024]{0,2,1:T(8,128)(2,1)S(1)} %fusion.12), kind=kOutput, calls=%fused_computation | convolution fusion | flops 1879048192 | bytes 11534336 | tf_op jit(solution)/shard_map/dot_general | solution.py:46
  75.3 7.1 %fusion.9 = f32[256,3584]{1,0:T(8,128)} fusion(f32[256,3584]{1,0:T(8,128)S(1)} %fusion, bf16[3,1024,3584]{2,1,0:T(8,128)(2,1)} %param.10, bf16[256,2,1024]{0,2,1:T(8,128)(2,1)S(1)} %fusion.12), kind=kOutput, calls=%fused_computation.9 | convolution fusion | flops 1879965696 | bytes 15204352 | tf_op jit(solution)/shard_map/dot_general | solution.py:46
  82.4 0.0 reduce-scatter.5.cloned.1.call-update
  82.4 0.0 reduce-scatter.3.cloned.1.call-start
  82.5 7.0 %fusion.4 = f32[256,3584]{1,0:T(8,128)} fusion(bf16[3,1024,3584]{2,1,0:T(8,128)(2,1)} %param.10, bf16[256,2,1024]{0,2,1:T(8,128)(2,1)S(1)} %fusion.12), kind=kOutput, calls=%fused_computation.4 | convolution fusion | flops 1879048192 | bytes 11534336 | tf_op jit(solution)/shard_map/dot_general | solution.py:46
  89.5 0.0 copy-start
  89.5 0.0 reduce-scatter.3.cloned.1.call-update
  89.5 60.7 %reduce-scatter.5.cloned.1.call-done = f32[16,3584]{1,0:T(8,128)} async-done(((f32[256,3584]{1,0:T(8,128)}), f32[16,3584]{1,0:T(8,128)}) %reduce-scatter.5.cloned.1.call-update) | async-done | bytes 229392 | tf_op jit(solution)/shard_map/reduce_scatter | solution.py:64
  150.2 71.8 %reduce-scatter.3.cloned.1.call-done = f32[16,3584]{1,0:T(8,128)} async-done(((f32[256,3584]{1,0:T(8,128)}), f32[16,3584]{1,0:T(8,128)}) %reduce-scatter.3.cloned.1.call-update) | async-done | bytes 229392 | tf_op jit(solution)/shard_map/reduce_scatter | solution.py:64
  222.0 0.0 copy-done
  222.0 1.1 fusion.13
  223.1 0.9 copy.13
  (2 shorter events, 0.0 us)
Async XLA Ops:
  6.5 53.4 %all-gather.2.cloned.1.call-start = ((), (), s32[]{:S(2)}) async-start(), calls=%async_computation.2 | async-start | bytes 3899392 | tf_op jit(solution)/shard_map/all_gather | solution.py:58
  8.2 142.0 %reduce-scatter.5.cloned.1.call-start = ((), (), s32[]{:S(2)}) async-start(), calls=%async_computation.4 | async-start | bytes 3899392 | tf_op jit(solution)/shard_map/reduce_scatter | solution.py:64
  82.4 139.6 %reduce-scatter.3.cloned.1.call-start = ((), (), s32[]{:S(2)}) async-start(), calls=%async_computation.3 | async-start | bytes 3899392 | tf_op jit(solution)/shard_map/reduce_scatter | solution.py:64
  89.5 132.5 %copy-start = (f32[2,3584]{1,0:T(2,128)S(1)}, f32[2,3584]{1,0:T(2,128)}, u32[]{:S(2)}) copy-start(f32[2,3584]{1,0:T(2,128)} %param.11) | copy-start | bytes 86020
Sparse Core Ops, SparseCore 0:
  9.6 50.2 all-gather.1
  82.6 67.6 reduce-scatter.4
  154.6 67.3 reduce-scatter.2
where the time goes:
time: 231 us
  waiting for transfers between devices  182 us (79%)
  matrix products  29.7 us (13%)
  between operations  13.2 us (6%)
  other arithmetic  2.81 us (1%)
  local copies, waits for them, and re-layouts  2.58 us (1%)
    reduce_scatter x2, waiting for transfers between devices, body(): lax.psum_scatter(layer_term(latent_codes, dec_weight, target, own_rows *...  133 us
    all_gather x1, waiting for transfers between devices, body(): lax.all_gather(residuals, 'lat', axis=0, tiled=True)  49.7 us
    dot_general x3, matrix products, layer_term(): jnp.dot(latent_codes[:, source, :], dec_weight[pair_index(source, target)...  19.3 us
    dot_general x1, matrix products, encode(): jnp.einsum('rld,ldk->rlk', fragment, enc_weight, preferred_element_type=j...  10.2 us
  transfers between devices with their start and end apart: 3, of which 3 were waited for; matrix products, arithmetic and copies ran while one was open for 4% of the time, Pallas kernels for 0%

commit v1 on v0

--- a/solution.py
+++ b/solution.py
@@ -1,15 +1,400 @@
+import functools
+
 import jax
 import jax.numpy as jnp
 from jax import lax
+from jax.experimental import pallas as pl
+from jax.experimental.pallas import tpu as pltpu
 from jax.sharding import PartitionSpec as P
 
 BLOCK = 128
 LAYERS = 2
 TILE = 64
+CORES = 2
+YS = 2
+CHUNK = 256
+HALVES = 2
+MESH = pl.DeviceIdType.MESH
 
 
 def pair_index(source, target):
     return source * LAYERS - source * (source - 1) // 2 + target - source
+
+
+def fused(
+    zs, x_ref, ew_hbm, eb_ref, dw_hbm, db_ref, ab_ref, ac_ref, o_ref,
+    ew, dw, xg, codes, mask, acc, csend, crecv, ysend, yrecv, zsend, zrecv,
+    w_sem, up_sem, down_sem, y_sem, core_sem, got_sem,
+    cs_sem, cr_sem, ys_sem, yr_sem, zs_sem, zr_sem,
+):
+    layers, rows, width = x_ref.shape
+    lat_here = ew.shape[2]
+    seg_cols = acc.shape[2]
+    half = width // seg_cols
+    plane = zs * rows
+    kept = YS * plane
+    f32, bf16 = jnp.float32, jnp.bfloat16
+
+    rep = lax.axis_index("rep")
+    me = lax.axis_index("lat")
+    core = lax.rem(me, CORES)
+    y = lax.rem(me // CORES, YS)
+    z = me // (CORES * YS)
+
+    def device(z_at, y_at, core_at):
+        return (rep, (z_at * YS + y_at) * CORES + core_at)
+
+    up, down = device(z + 1, y, core), device(z - 1, y, core)
+    across, twin = device(z, 1 - y, core), device(z, y, 1 - core)
+    has_up, has_down = z < zs - 1, z > 0
+
+    barrier = pltpu.get_barrier_semaphore()
+    for peer in (across, twin):
+        pl.semaphore_signal(barrier, inc=1, device_id=peer, device_id_type=MESH)
+
+    @pl.when(has_up)
+    def _():
+        pl.semaphore_signal(barrier, inc=1, device_id=up, device_id_type=MESH)
+
+    @pl.when(has_down)
+    def _():
+        pl.semaphore_signal(barrier, inc=1, device_id=down, device_id_type=MESH)
+
+    def weight_copies():
+        copies = [pltpu.make_async_copy(ew_hbm.at[l], ew.at[l], w_sem.at[l]) for l in range(layers)]
+        copies += [
+            pltpu.make_async_copy(dw_hbm.at[p], dw.at[p], w_sem.at[layers + p])
+            for p in range(dw.shape[0])
+        ]
+        return copies
+
+    weights = weight_copies()
+    order = [0, layers, 1] + [layers + p for p in range(1, dw.shape[0])]
+    for i in order:
+        weights[i].start()
+
+    for l in range(layers):
+        xg[l, pl.ds(pl.multiple_of(z * rows, rows), rows), :] = x_ref[l]
+
+    pl.semaphore_wait(
+        barrier, 2 + jnp.where(has_up, 1, 0) + jnp.where(has_down, 1, 0)
+    )
+
+    def at(l, slot):
+        return xg.at[l, pl.ds(pl.multiple_of(slot * rows, rows), rows), :]
+
+    def gather_copy(l, slot, to_slot, peer, send_sem):
+        return pltpu.make_async_remote_copy(
+            src_ref=at(l, slot), dst_ref=at(l, to_slot), send_sem=send_sem,
+            recv_sem=got_sem.at[l, to_slot], device_id=peer, device_id_type=MESH,
+        )
+
+    def up_copy(l, zb):
+        return gather_copy(l, zb, zb, up, up_sem.at[l, zb])
+
+    def down_copy(l, zb):
+        return gather_copy(l, zb, zb, down, down_sem.at[l, zb])
+
+    def y_copy(l, zb):
+        return gather_copy(l, zb, zs + zb, across, y_sem.at[l, zb])
+
+    def core_copy(l, slot):
+        return gather_copy(l, slot, 2 * zs + slot, twin, core_sem.at[l, slot])
+
+    def got(l, slot):
+        pltpu.make_async_remote_copy(
+            src_ref=at(l, slot), dst_ref=at(l, slot), send_sem=core_sem.at[l, 0],
+            recv_sem=got_sem.at[l, slot], device_id=twin, device_id_type=MESH,
+        ).wait_recv()
+
+    def own(l):
+        y_copy(l, z).start()
+
+        @pl.when(has_up)
+        def _():
+            up_copy(l, z).start()
+
+        @pl.when(has_down)
+        def _():
+            down_copy(l, z).start()
+
+        core_copy(l, z).start()
+
+    def step(l, s):
+        @pl.when(z >= s)
+        def _():
+            zb = z - s
+            got(l, zb)
+
+            @pl.when(has_up)
+            def _():
+                up_copy(l, zb).start()
+
+            y_copy(l, zb).start()
+            core_copy(l, zb).start()
+
+        @pl.when(z + s < zs)
+        def _():
+            zb = z + s
+            got(l, zb)
+
+            @pl.when(has_down)
+            def _():
+                down_copy(l, zb).start()
+
+            y_copy(l, zb).start()
+            core_copy(l, zb).start()
+
+    def y_forward(l, s):
+        @pl.when(z >= s)
+        def _():
+            got(l, zs + z - s)
+            core_copy(l, zs + z - s).start()
+
+        if s:
+            @pl.when(z + s < zs)
+            def _():
+                got(l, zs + z + s)
+                core_copy(l, zs + z + s).start()
+
+    def y_forwards(l):
+        for s in range(zs):
+            y_forward(l, s)
+
+    def core_gets(l):
+        for slot in range(2 * zs, 4 * zs):
+            got(l, slot)
+
+    def make_mask():
+        for l in range(layers):
+            listed = ab_ref[l]
+            tile = lax.broadcasted_iota(jnp.int32, listed.shape, 0)
+            place = lax.broadcasted_iota(jnp.int32, listed.shape, 1)
+            count = jnp.zeros(listed.shape, jnp.int32)
+            for t in range(zs):
+                count = jnp.where(tile == t, ac_ref[l, t], count)
+            used = place < count
+            blocks_here = lat_here // BLOCK
+            for j in range(blocks_here):
+                hit = jnp.where(used & (listed == me * blocks_here + j), 1.0, 0.0)
+                hit = jnp.max(hit, axis=1, keepdims=True)
+                for t in range(zs):
+                    mask[l, t * rows : (t + 1) * rows, j * BLOCK : (j + 1) * BLOCK] = (
+                        jnp.broadcast_to(hit[t : t + 1], (rows, BLOCK))
+                    )
+
+    def encode(l, first, last):
+        @pl.loop(first, last)
+        def _(n):
+            cols = pl.ds(pl.multiple_of(n * CHUNK, CHUNK), CHUNK)
+            pre = jnp.dot(xg[l], ew[l, :, cols], preferred_element_type=f32)
+            pre = jnp.maximum(pre + eb_ref[l : l + 1, cols], 0.0)
+            pre = pre.reshape(CORES * YS, plane, CHUNK) * mask[l, :, cols][None]
+            codes[l, :, cols] = pre.reshape(CORES * kept, CHUNK).astype(bf16)
+
+    def decode(seg):
+        m, h = seg // half, seg % half
+
+        @pl.loop(0, seg_cols // CHUNK)
+        def _(j):
+            cols = pl.ds(pl.multiple_of(h * seg_cols + j * CHUNK, CHUNK), CHUNK)
+            to = pl.ds(pl.multiple_of(j * CHUNK, CHUNK), CHUNK)
+            total = None
+            for l in range(m + 1):
+                term = jnp.dot(
+                    codes[l], dw[pair_index(l, m), :, cols], preferred_element_type=f32
+                )
+                total = term if total is None else total + term
+            acc[seg, :, to] = total[:kept]
+            csend[seg, :, to] = total[kept:].astype(bf16)
+
+        core_sum(seg).start()
+
+    def core_sum(seg):
+        return pltpu.make_async_remote_copy(
+            src_ref=csend.at[seg], dst_ref=crecv.at[seg], send_sem=cs_sem.at[seg],
+            recv_sem=cr_sem.at[seg], device_id=twin, device_id_type=MESH,
+        )
+
+    def y_sum(seg):
+        return pltpu.make_async_remote_copy(
+            src_ref=ysend.at[seg], dst_ref=yrecv.at[seg], send_sem=ys_sem.at[seg],
+            recv_sem=yr_sem.at[seg], device_id=across, device_id_type=MESH,
+        )
+
+    def z_sum(seg, way, d):
+        part = pl.ds(pl.multiple_of(d * rows, rows), rows)
+        return pltpu.make_async_remote_copy(
+            src_ref=zsend.at[seg, part], dst_ref=zrecv.at[seg, way, part],
+            send_sem=zs_sem.at[seg, d], recv_sem=zr_sem.at[seg, way, d],
+            device_id=(up, down)[way], device_id_type=MESH,
+        )
+
+    def after_core(seg):
+        core_sum(seg).wait_recv()
+        ysend[seg] = (acc[seg, plane:] + crecv[seg, plane:].astype(f32)).astype(bf16)
+        y_sum(seg).start()
+        acc[seg, :plane] = acc[seg, :plane] + crecv[seg, :plane].astype(f32)
+
+    def after_y(seg):
+        y_sum(seg).wait_recv()
+        acc[seg, :plane] = acc[seg, :plane] + yrecv[seg].astype(f32)
+
+    def take(seg, way, d):
+        part = pl.ds(pl.multiple_of(d * rows, rows), rows)
+        z_sum(seg, way, d).wait_recv()
+        acc[seg, part] = acc[seg, part] + zrecv[seg, way, part].astype(f32)
+
+    def z_hop(seg, way, d):
+        part = pl.ds(d * rows, rows)
+        going, chained = ((z < d, has_down), (z > d, has_up))[way]
+
+        @pl.when(going)
+        def _():
+            @pl.when(chained)
+            def _():
+                take(seg, way, d)
+
+            zsend[seg, part] = acc[seg, part].astype(bf16)
+            z_sum(seg, way, d).start()
+
+    def z_hops(seg):
+        for i in range(1, zs):
+            z_hop(seg, 0, zs - i)
+            z_hop(seg, 1, i - 1)
+
+    def finish(seg):
+        @pl.when(has_down)
+        def _():
+            take(seg, 0, z)
+
+        @pl.when(has_up)
+        def _():
+            take(seg, 1, z)
+
+        m, h = seg // half, seg % half
+        cols = slice(h * seg_cols, (h + 1) * seg_cols)
+        own_rows = pl.ds(pl.multiple_of(z * rows, rows), rows)
+        o_ref[m, :, cols] = (acc[seg, own_rows] + db_ref[m : m + 1, cols]).astype(bf16)
+
+    chunks = lat_here // CHUNK
+    mid = (chunks + 1) // 2
+    own(0)
+    make_mask()
+    step(0, 1)
+    step(0, 2)
+    own(1)
+    step(0, 3)
+    y_forwards(0)
+    step(1, 1)
+    core_gets(0)
+    weights[0].wait()
+    encode(0, 0, mid)
+    step(1, 2)
+    encode(0, mid, chunks)
+    step(1, 3)
+    weights[layers].wait()
+    decode(0)
+    y_forwards(1)
+    after_core(0)
+    decode(1)
+    core_gets(1)
+    after_core(1)
+    weights[1].wait()
+    encode(1, 0, chunks)
+    after_y(0)
+    for p in range(1, dw.shape[0]):
+        weights[layers + p].wait()
+    decode(2)
+    after_y(1)
+    after_core(2)
+    z_hops(0)
+    decode(3)
+    z_hops(1)
+    after_core(3)
+    finish(0)
+    after_y(2)
+    z_hops(2)
+    finish(1)
+    after_y(3)
+    z_hops(3)
+    finish(2)
+    finish(3)
+
+    for l in range(layers):
+        for zb in range(zs):
+            @pl.when(has_up & (z >= zb))
+            def _():
+                up_copy(l, zb).wait_send()
+
+            @pl.when(has_down & (z <= zb))
+            def _():
+                down_copy(l, zb).wait_send()
+
+            y_copy(l, zb).wait_send()
+        for slot in range(2 * zs):
+            core_copy(l, slot).wait_send()
+    for seg in range(layers * half):
+        core_sum(seg).wait_send()
+        y_sum(seg).wait_send()
+        for d in range(zs):
+            for way in range(2):
+                @pl.when((z < d, z > d)[way])
+                def _():
+                    z_sum(seg, way, d).wait_send()
+
+
+def body_fused(zs, residuals, enc_weight, enc_bias, dec_weight, dec_bias, active_blocks, active_counts):
+    rows, layers, width = residuals.shape
+    lat_here = enc_weight.shape[2]
+    pairs = dec_weight.shape[0]
+    segs, seg_cols = layers * HALVES, width // HALVES
+    slots = CORES * YS * zs
+    plane = zs * rows
+    kept = YS * plane
+    bf16, f32 = jnp.bfloat16, jnp.float32
+    vmem = pl.BlockSpec(memory_space=pltpu.VMEM)
+    hbm = pl.BlockSpec(memory_space=pl.ANY)
+    dma = pltpu.SemaphoreType.DMA
+    out = pl.pallas_call(
+        functools.partial(fused, zs),
+        out_shape=jax.ShapeDtypeStruct((layers, rows, width), bf16),
+        in_specs=[vmem, hbm, vmem, hbm, vmem, vmem, pl.BlockSpec(memory_space=pltpu.SMEM)],
+        out_specs=vmem,
+        scratch_shapes=[
+            pltpu.VMEM((layers, width, lat_here), bf16),
+            pltpu.VMEM((pairs, lat_here, width), bf16),
+            pltpu.VMEM((layers, slots * rows, width), bf16),
+            pltpu.VMEM((layers, slots * rows, lat_here), bf16),
+            pltpu.VMEM((layers, plane, lat_here), f32),
+            pltpu.VMEM((segs, kept, seg_cols), f32),
+            pltpu.VMEM((segs, kept, seg_cols), bf16),
+            pltpu.VMEM((segs, kept, seg_cols), bf16),
+            pltpu.VMEM((segs, plane, seg_cols), bf16),
+            pltpu.VMEM((segs, plane, seg_cols), bf16),
+            pltpu.VMEM((segs, plane, seg_cols), bf16),
+            pltpu.VMEM((segs, 2, plane, seg_cols), bf16),
+            dma((layers + pairs,)),
+            dma((layers, zs)),
+            dma((layers, zs)),
+            dma((layers, zs)),
+            dma((layers, 2 * zs)),
+            dma((layers, slots)),
+            dma((segs,)),
+            dma((segs,)),
+            dma((segs,)),
+            dma((segs,)),
+            dma((segs, zs)),
+            dma((segs, 2, zs)),
+        ],
+        compiler_params=pltpu.CompilerParams(
+            collective_id=0, has_side_effects=True, vmem_limit_bytes=61 * 2**20
+        ),
+    )(
+        residuals.transpose(1, 0, 2), enc_weight, enc_bias, dec_weight, dec_bias,
+        active_blocks, active_counts,
+    )
+    return out.transpose(1, 0, 2)
 
 
 def block_table(active_blocks, active_counts, blocks_here):
@@ -73,8 +458,17 @@
 
 
 def solution(mesh):
+    lat = mesh.shape["lat"]
+
+    def either(residuals, enc_weight, *rest):
+        rows = residuals.shape[0]
+        zs = lat // (CORES * YS)
+        whole = zs == 4 and rows % 16 == 0 and rows * CORES * YS == TILE
+        part = functools.partial(body_fused, zs) if whole else body
+        return part(residuals, enc_weight, *rest)
+
     return jax.shard_map(
-        body,
+        either,
         mesh=mesh,
         in_specs=(
             P(("rep", "lat"), None, None),

time: 231 us -> 87.3 us (0.38)
  waiting for transfers between devices: 182 us -> 0 us
  Pallas kernels: 0 us -> 83.6 us
  matrix products: 29.7 us -> 0 us
  between operations: 13.2 us -> 0.01 us
  other arithmetic: 2.81 us -> 0 us
    reduce_scatter x2 -> x0, waiting for transfers between devices: 133 us -> none  [body(): lax.psum_scatter(layer_term(latent_codes, dec_weight, target, own_rows *...]
    pallas_call x0 -> x1, Pallas kernels: none -> 83.6 us  [body_fused(): pl.pallas_call(functools.partial(fused, zs), out_shape=jax.ShapeDtypeStru...]
    all_gather x1 -> x0, waiting for transfers between devices: 49.7 us -> none  [body(): lax.all_gather(residuals, 'lat', axis=0, tiled=True)]
    dot_general x5 -> x0, matrix products: 29.7 us -> none  [the longest x3 19.3 us: layer_term(): jnp.dot(latent_codes[:, source, :], dec_weight[pair_index(source, target)...]
  transfers between devices with their start and end apart: 3 -> 0, of which waited for: 3 -> 0; matrix products, arithmetic and copies ran while one was open for 4% -> 0% of each run, Pallas kernels for 0% -> 0%
where the time goes in v1:
time: 87.3 us; the launch traced here: 87.1 us
  Pallas kernels  83.6 us (96%)
  local copies, waits for them, and re-layouts  3.51 us (4%)
    pallas_call x1, Pallas kernels, body_fused(): pl.pallas_call(functools.partial(fused, zs), out_shape=jax.ShapeDtypeStru...  83.6 us
    transpose x1, local copies, waits for them, and re-layouts, body_fused(): return out.transpose(1, 0, 2)  1.86 us

profile of v1, /device:TPU:0, one launch (start us, length us, event | category | flops | bytes accessed | tf_op | source)
XLA Modules:
  0.0 87.1 jit_solution(16375228074105253863)
XLA Ops:
  0.0 1.6 %copy.11 = bf16[16,2,3584]{2,0,1:T(8,128)(2,1)} copy(bf16[16,2,3584]{2,1,0:T(2,128)(2,1)} %param.7) | data formatting | bytes 458752 | tf_op args[0]
  1.7 83.6 %shard_map.73 = bf16[2,16,3584]{2,1,0:T(8,128)(2,1)} custom-call(bf16[2,16,3584]{2,1,0:T(8,128)(2,1)} %bitcast.5, bf16[2,3584,1024]{2,1,0:T(8,128)(2,1)} %ew_hbm.1, f32[2,1024]{1,0:T(2,128)} %eb_ref.1, bf16[3,1024,3584]{2,1,0:T(8,128)(2,1)} %dw_hbm.1, f32[2,3584]{1,0:T(2,128)} %db_ref.1, s32[2,4,32]{2,1,0:T(4,128)} %ab_ref.1, s32[2,4]{1,0:T(2,128)} %ac_ref.1), custom_call_target="tpu_custom_call" | custom-call | tf_op jit(solution)/shard_map/pallas_call | solution.py:359
  85.2 1.9 %copy.9 = bf16[16,2,3584]{2,1,0:T(2,128)(2,1)} copy(bf16[16,2,3584]{2,0,1:T(8,128)(2,1)} %bitcast.4) | data formatting | bytes 458752 | tf_op jit(solution)/shard_map/transpose | solution.py:397

commit v2 on v1

v2 whole, which is shorter than its diff:
```python
import functools

import jax
import jax.numpy as jnp
from jax import lax
from jax.experimental import pallas as pl
from jax.experimental.pallas import tpu as pltpu
from jax.sharding import PartitionSpec as P

BLOCK = 128
LAYERS = 2
TILE = 64
CORES = 2
YS = 2
CHUNK = 256
PIECES = ((0, 0, 2), (0, 1, 2), (1, 0, 2), (1, 1, 2))
SEGS = ((0, 0, 7), (0, 7, 7), (1, 0, 7), (1, 7, 7))
MESH = pl.DeviceIdType.MESH


def pair_index(source, target):
    return source * LAYERS - source * (source - 1) // 2 + target - source


def fused(
    zs, x_ref, ew_hbm, eb_ref, dw_hbm, db_ref, ab_ref, ac_ref, o_ref,
    ew, dw, xg, codes, mask, acc, csend, crecv, ysend, yrecv, zsend, zrecv,
    w_sem, line_sem, y_sem, core_sem, got_sem,
    cs_sem, cr_sem, ys_sem, yr_sem, zs_sem, zr_sem,
):
    layers, rows, width = x_ref.shape
    lat_here = ew.shape[2]
    plane = zs * rows
    kept = YS * plane
    f32, bf16 = jnp.float32, jnp.bfloat16

    rep = lax.axis_index("rep")
    me = lax.axis_index("lat")
    core = lax.rem(me, CORES)
    y = lax.rem(me // CORES, YS)
    z = me // (CORES * YS)

    def device(z_at, y_at, core_at):
        return (rep, (z_at * YS + y_at) * CORES + core_at)

    across, twin = device(z, 1 - y, core), device(z, y, 1 - core)

    def other(k):
        return (z + 1 - 2 * lax.rem(z, 2), lax.rem(z + 2, 4), 3 - z)[k]

    barrier = pltpu.get_barrier_semaphore()
    for peer in (across, twin, *(device(other(k), y, core) for k in range(3))):
        pl.semaphore_signal(barrier, inc=1, device_id=peer, device_id_type=MESH)

    def weight_copies():
        copies = [pltpu.make_async_copy(ew_hbm.at[l], ew.at[l], w_sem.at[l]) for l in range(layers)]
        copies += [
            pltpu.make_async_copy(dw_hbm.at[p], dw.at[p], w_sem.at[layers + p])
            for p in range(dw.shape[0])
        ]
        return copies

    weights = weight_copies()
    order = [0, layers, 1] + [layers + p for p in range(1, dw.shape[0])]
    for i in order:
        weights[i].start()

    for l in range(layers):
        xg[l, pl.ds(pl.multiple_of(z * rows, rows), rows), :] = x_ref[l]

    pl.semaphore_wait(barrier, 5)

    def at(q, slot):
        l, part, parts = PIECES[q]
        cols = width // parts
        return xg.at[
            l, pl.ds(pl.multiple_of(slot * rows, rows), rows), part * cols : (part + 1) * cols
        ]

    def gather_copy(q, slot, to_slot, peer, send_sem):
        return pltpu.make_async_remote_copy(
            src_ref=at(q, slot), dst_ref=at(q, to_slot), send_sem=send_sem,
            recv_sem=got_sem.at[q, to_slot], device_id=peer, device_id_type=MESH,
        )

    def line_copy(q, k):
        return gather_copy(q, z, z, device(other(k), y, core), line_sem.at[q, k])

    def y_copy(q, zb):
        return gather_copy(q, zb, zs + zb, across, y_sem.at[q, zb])

    def core_copy(q, slot):
        return gather_copy(q, slot, 2 * zs + slot, twin, core_sem.at[q, slot])

    def got(q, slot):
        pltpu.make_async_remote_copy(
            src_ref=at(q, slot), dst_ref=at(q, slot), send_sem=core_sem.at[q, 0],
            recv_sem=got_sem.at[q, slot], device_id=twin, device_id_type=MESH,
        ).wait_recv()

    def own(q):
        for k in reversed(range(3)):
            line_copy(q, k).start()
        y_copy(q, z).start()
        core_copy(q, z).start()

    def step(q, k):
        got(q, other(k))
        y_copy(q, other(k)).start()
        core_copy(q, other(k)).start()

    def y_forward(q, k):
        zb = z if k < 0 else other(k)
        got(q, zs + zb)
        core_copy(q, zs + zb).start()

    def core_gets(q):
        for slot in range(2 * zs, 4 * zs):
            got(q, slot)

    def make_mask():
        for l in range(layers):
            listed = ab_ref[l]
            tile = lax.broadcasted_iota(jnp.int32, listed.shape, 0)
            place = lax.broadcasted_iota(jnp.int32, listed.shape, 1)
            count = jnp.zeros(listed.shape, jnp.int32)
            for t in range(zs):
                count = jnp.where(tile == t, ac_ref[l, t], count)
            used = place < count
            blocks_here = lat_here // BLOCK
            for j in range(blocks_here):
                hit = jnp.where(used & (listed == me * blocks_here + j), 1.0, 0.0)
                hit = jnp.max(hit, axis=1, keepdims=True)
                for t in range(zs):
                    mask[l, t * rows : (t + 1) * rows, j * BLOCK : (j + 1) * BLOCK] = (
                        jnp.broadcast_to(hit[t : t + 1], (rows, BLOCK))
                    )

    def encode(l, first, last):
        @pl.loop(first, last)
        def _(n):
            cols = pl.ds(pl.multiple_of(n * CHUNK, CHUNK), CHUNK)
            pre = jnp.dot(xg[l], ew[l, :, cols], preferred_element_type=f32)
            pre = jnp.maximum(pre + eb_ref[l : l + 1, cols], 0.0)
            pre = pre.reshape(CORES * YS, plane, CHUNK) * mask[l, :, cols][None]
            codes[l, :, cols] = pre.reshape(CORES * kept, CHUNK).astype(bf16)

    def place(seg):
        m, first, count = SEGS[seg]
        return m * width + first * CHUNK, count * CHUNK

    def span(seg):
        return pl.ds(*place(seg))

    def rows_of(d):
        return pl.ds(pl.multiple_of(d * rows, rows), rows)

    def decode(seg):
        m, first, count = SEGS[seg]

        @pl.loop(first, first + count)
        def _(j):
            cols = pl.ds(pl.multiple_of(j * CHUNK, CHUNK), CHUNK)
            to = pl.ds(pl.multiple_of(m * width + j * CHUNK, CHUNK), CHUNK)
            total = None
            for l in range(m + 1):
                term = jnp.dot(
                    codes[l], dw[pair_index(l, m), :, cols], preferred_element_type=f32
                )
                total = term if total is None else total + term
            acc[:, to] = total[:kept]
            csend[:, to] = total[kept:].astype(bf16)

        core_sum(seg).start()

    def core_sum(seg):
        return pltpu.make_async_remote_copy(
            src_ref=csend.at[:, span(seg)], dst_ref=crecv.at[:, span(seg)],
            send_sem=cs_sem.at[seg], recv_sem=cr_sem.at[seg],
            device_id=twin, device_id_type=MESH,
        )

    def y_sum(seg):
        return pltpu.make_async_remote_copy(
            src_ref=ysend.at[:, span(seg)], dst_ref=yrecv.at[:, span(seg)],
            send_sem=ys_sem.at[seg], recv_sem=yr_sem.at[seg],
            device_id=across, device_id_type=MESH,
        )

    def z_sum(seg, k):
        return pltpu.make_async_remote_copy(
            src_ref=zsend.at[rows_of(other(k)), span(seg)], dst_ref=zrecv.at[k, :, span(seg)],
            send_sem=zs_sem.at[seg, k], recv_sem=zr_sem.at[seg, k],
            device_id=device(other(k), y, core), device_id_type=MESH,
        )

    def after_core(seg):
        core_sum(seg).wait_recv()
        cols = span(seg)
        ysend[:, cols] = (acc[plane:, cols] + crecv[plane:, cols].astype(f32)).astype(bf16)
        y_sum(seg).start()
        acc[:plane, cols] = acc[:plane, cols] + crecv[:plane, cols].astype(f32)

    def after_y(seg):
        y_sum(seg).wait_recv()
        cols = span(seg)
        total = acc[:plane, cols] + yrecv[:, cols].astype(f32)
        zsend[:, cols] = total.astype(bf16)
        for k in reversed(range(3)):
            z_sum(seg, k).start()
        acc[:plane, cols] = total

    def finish(seg):
        m, first, count = SEGS[seg]
        cols = span(seg)
        own_cols = slice(first * CHUNK, (first + count) * CHUNK)
        total = acc[rows_of(z), cols] + db_ref[m : m + 1, own_cols]
        for k in range(3):
            z_sum(seg, k).wait_recv()
            total = total + zrecv[k, :, cols].astype(f32)
        o_ref[m, :, own_cols] = total.astype(bf16)

    chunks = lat_here // CHUNK
    mid = (chunks + 1) // 2
    own(0)
    own(1)
    make_mask()
    for q in range(2):
        for k in range(3):
            step(q, k)
    own(2)
    own(3)
    for q in range(2):
        for k in range(-1, 3):
            y_forward(q, k)
    for k in range(3):
        step(2, k)
    for k in range(3):
        step(3, k)
    core_gets(0)
    core_gets(1)
    weights[0].wait()
    encode(0, 0, mid)
    for k in range(-1, 3):
        y_forward(2, k)
    encode(0, mid, chunks)
    weights[layers].wait()
    decode(0)
    for k in range(-1, 3):
        y_forward(3, k)
    after_core(0)
    decode(1)
    core_gets(2)
    core_gets(3)
    after_core(1)
    weights[1].wait()
    encode(1, 0, chunks)
    after_y(0)
    for p in range(1, dw.shape[0]):
        weights[layers + p].wait()
    decode(2)
    after_y(1)
    decode(3)
    after_core(2)
    after_core(3)
    finish(0)
    finish(1)
    after_y(2)
    after_y(3)
    finish(2)
    finish(3)

    for q in range(len(PIECES)):
        for k in range(3):
            line_copy(q, k).wait_send()
        for zb in range(zs):
            y_copy(q, zb).wait_send()
        for slot in range(2 * zs):
            core_copy(q, slot).wait_send()
    for seg in range(len(SEGS)):
        core_sum(seg).wait_send()
        y_sum(seg).wait_send()
        for k in range(3):
            z_sum(seg, k).wait_send()


def body_fused(zs, residuals, enc_weight, enc_bias, dec_weight, dec_bias, active_blocks, active_counts):
    rows, layers, width = residuals.shape
    lat_here = enc_weight.shape[2]
    pairs = dec_weight.shape[0]
    pieces, segs, total = len(PIECES), len(SEGS), layers * width
    slots = CORES * YS * zs
    plane = zs * rows
    kept = YS * plane
    bf16, f32 = jnp.bfloat16, jnp.float32
    vmem = pl.BlockSpec(memory_space=pltpu.VMEM)
    hbm = pl.BlockSpec(memory_space=pl.ANY)
    dma = pltpu.SemaphoreType.DMA
    out = pl.pallas_call(
        functools.partial(fused, zs),
        out_shape=jax.ShapeDtypeStruct((layers, rows, width), bf16),
        in_specs=[vmem, hbm, vmem, hbm, vmem, vmem, pl.BlockSpec(memory_space=pltpu.SMEM)],
        out_specs=vmem,
        scratch_shapes=[
            pltpu.VMEM((layers, width, lat_here), bf16),
            pltpu.VMEM((pairs, lat_here, width), bf16),
            pltpu.VMEM((layers, slots * rows, width), bf16),
            pltpu.VMEM((layers, slots * rows, lat_here), bf16),
            pltpu.VMEM((layers, plane, lat_here), f32),
            pltpu.VMEM((kept, total), f32),
            pltpu.VMEM((kept, total), bf16),
            pltpu.VMEM((kept, total), bf16),
            pltpu.VMEM((plane, total), bf16),
            pltpu.VMEM((plane, total), bf16),
            pltpu.VMEM((plane, total), bf16),
            pltpu.VMEM((3, rows, total), bf16),
            dma((layers + pairs,)),
            dma((pieces, 3)),
            dma((pieces, zs)),
            dma((pieces, 2 * zs)),
            dma((pieces, slots)),
            dma((segs,)),
            dma((segs,)),
            dma((segs,)),
            dma((segs,)),
            dma((segs, 3)),
            dma((segs, 3)),
        ],
        compiler_params=pltpu.CompilerParams(
            collective_id=0, has_side_effects=True, vmem_limit_bytes=61 * 2**20
        ),
    )(
        residuals.transpose(1, 0, 2), enc_weight, enc_bias, dec_weight, dec_bias,
        active_blocks, active_counts,
    )
    return out.transpose(1, 0, 2)


def block_table(active_blocks, active_counts, blocks_here):
    holder = lax.axis_index("lat")
    block_ids = holder * blocks_here + jnp.arange(blocks_here, dtype=jnp.int32)
    in_list = (
        jnp.arange(active_blocks.shape[2], dtype=jnp.int32)[None, None, :]
        < active_counts[:, :, None]
    )
    matched = (active_blocks[..., None] == block_ids) & in_list[..., None]
    return jnp.any(matched, axis=2).astype(jnp.float32)


def encode(fragment, enc_weight, enc_bias, table):
    row_count = fragment.shape[0]
    lat_here = enc_weight.shape[2]
    blocks_here = lat_here // BLOCK
    preact = jnp.einsum("rld,ldk->rlk", fragment, enc_weight, preferred_element_type=jnp.float32)
    preact = preact + enc_bias[None, :, :]
    tile_of = jnp.arange(row_count, dtype=jnp.int32) // TILE
    one_hot = (tile_of[:, None] == jnp.arange(table.shape[1], dtype=jnp.int32)[None, :]).astype(
        jnp.float32
    )
    keep_rows = jnp.einsum("rt,ltj->rlj", one_hot, table)
    activation = (
        jax.nn.relu(preact).reshape(row_count, LAYERS, blocks_here, BLOCK) * keep_rows[..., None]
    )
    return activation.reshape(row_count, LAYERS, lat_here).astype(jnp.bfloat16)


def layer_term(latent_codes, dec_weight, target, amount):
    summed = jnp.zeros((amount, dec_weight.shape[2]), jnp.float32)
    for source in range(target + 1):
        summed = summed + jnp.dot(
            latent_codes[:, source, :],
            dec_weight[pair_index(source, target)],
            preferred_element_type=jnp.float32,
        )
    return summed


def body(residuals, enc_weight, enc_bias, dec_weight, dec_bias, active_blocks, active_counts):
    blocks_here = enc_weight.shape[2] // BLOCK
    table = block_table(active_blocks, active_counts, blocks_here)
    latent_codes = encode(
        lax.all_gather(residuals, "lat", axis=0, tiled=True), enc_weight, enc_bias, table
    )
    own_rows = latent_codes.shape[0] // lax.axis_size("lat")
    layers_out = []
    for target in range(LAYERS):
        layers_out.append(
            lax.psum_scatter(
                layer_term(latent_codes, dec_weight, target, own_rows * lax.axis_size("lat")),
                "lat",
                scatter_dimension=0,
                tiled=True,
            )
        )
    summed = jnp.stack(layers_out, axis=1)
    return (summed + dec_bias[None, :, :]).astype(jnp.bfloat16)


def solution(mesh):
    lat = mesh.shape["lat"]

    def either(residuals, enc_weight, *rest):
        rows = residuals.shape[0]
        zs = lat // (CORES * YS)
        whole = zs == 4 and rows % 16 == 0 and rows * CORES * YS == TILE
        part = functools.partial(body_fused, zs) if whole else body
        return part(residuals, enc_weight, *rest)

    return jax.shard_map(
        either,
        mesh=mesh,
        in_specs=(
            P(("rep", "lat"), None, None),
            P(None, None, "lat"),
            P(None, "lat"),
            P(None, "lat", None),
            P(),
            P("rep", None, None),
            P("rep", None),
        ),
        out_specs=P(("rep", "lat"), None, None),
        check_vma=False,
    )
```

time: 87.3 us -> 73.2 us (0.84)
  Pallas kernels: 83.6 us -> 69.5 us
    pallas_call x1, Pallas kernels: 83.6 us -> 69.5 us  [body_fused(): pl.pallas_call(functools.partial(fused, zs), out_shape=jax.ShapeDtypeStru...]
where the time goes in v2:
time: 73.2 us; the launch traced here: 73 us
  Pallas kernels  69.5 us (95%)
  local copies, waits for them, and re-layouts  3.51 us (5%)
    pallas_call x1, Pallas kernels, body_fused(): pl.pallas_call(functools.partial(fused, zs), out_shape=jax.ShapeDtypeStru...  69.5 us
    transpose x1, local copies, waits for them, and re-layouts, body_fused(): return out.transpose(1, 0, 2)  1.86 us
    unnamed x1, local copies, waits for them, and re-layouts  1.65 us

profile of v2, /device:TPU:0, one launch (start us, length us, event | category | flops | bytes accessed | tf_op | source)
XLA Modules:
  0.0 73.0 jit_solution(5649986107974607051)
XLA Ops:
  0.0 1.6 %copy.11 = bf16[16,2,3584]{2,0,1:T(8,128)(2,1)} copy(bf16[16,2,3584]{2,1,0:T(2,128)(2,1)} %param.7) | data formatting | bytes 458752 | tf_op args[0]
  1.7 69.5 %shard_map.73 = bf16[2,16,3584]{2,1,0:T(8,128)(2,1)} custom-call(bf16[2,16,3584]{2,1,0:T(8,128)(2,1)} %bitcast.5, bf16[2,3584,1024]{2,1,0:T(8,128)(2,1)} %ew_hbm.1, f32[2,1024]{1,0:T(2,128)} %eb_ref.1, bf16[3,1024,3584]{2,1,0:T(8,128)(2,1)} %dw_hbm.1, f32[2,3584]{1,0:T(2,128)} %db_ref.1, s32[2,4,32]{2,1,0:T(4,128)} %ab_ref.1, s32[2,4]{1,0:T(2,128)} %ac_ref.1), custom_call_target="tpu_custom_call" | custom-call | tf_op jit(solution)/shard_map/pallas_call | solution.py:299
  71.1 1.9 %copy.9 = bf16[16,2,3584]{2,1,0:T(2,128)(2,1)} copy(bf16[16,2,3584]{2,0,1:T(8,128)(2,1)} %bitcast.4) | data formatting | bytes 458752 | tf_op jit(solution)/shard_map/transpose | solution.py:336
